TPU v7x, 512 devices: a whole 4x4x16 slice. The times are simulated.
512 devices in a mesh: section: 32 (over x, z_lo), fsdp: 16 (over y, z_hi, core).
Axes of the slice: x: 4, y: 4, z: 16 (z_hi: 2, z_lo: 8; z = z_hi * 8 + z_lo), core: 2. Of those that a mesh axis runs over, the one named last changes fastest.
Arguments:
- table: bfloat16 [128000, 3584], P(('section', 'fsdp')), may hold values from -6 to 6
- hidden_states: bfloat16 [128, 3584], P('fsdp', 'section'), may hold values from -52 to 52
- embed_cotangent: bfloat16 [128, 3584], P('fsdp', 'section'), may hold values from -6 to 6
- teacher_logits: bfloat16 [128000, 128], P(('section', 'fsdp')), may hold values from -28 to 216
- student_ids: int32 [128], replicated, may hold values from 0 to 127999
- loss_mask: int32 [128], replicated, may hold values 0 or 1
Outputs:
- table_grad: bfloat16 [128000, 3584], P(('section', 'fsdp'))
- state_grad: bfloat16 [128, 3584], P('fsdp', 'section')
- loss: float32 [], replicated
All inputs are finite; a program needn't handle non-finite values.
Results may differ from a plain program's by a relative error of at most 0.014.
Values may be sent and summed in bfloat16 or wider, within the bound.
A program may use at most 64 MiB of HBM per device.

v0:
```python
import jax
import jax.numpy as jnp
from jax import lax
from jax.sharding import PartitionSpec as P

CONTRACT_LAST = (((1,), (1,)), ((), ()))
CONTRACT_FIRST = (((0,), (0,)), ((), ()))


def shards(table, hidden_states, embed_cotangent, teacher_logits, student_ids, loss_mask):
    shard_rows = table.shape[0]
    first_row = lax.axis_index(("section", "fsdp")) * shard_rows
    columns = (
        lax.all_gather(hidden_states, "section", axis=1, tiled=True),
        lax.all_gather(embed_cotangent, "section", axis=1, tiled=True),
    )
    states, cotangent = (
        lax.all_gather(columns[0], "fsdp", axis=0, tiled=True),
        lax.all_gather(columns[1], "fsdp", axis=0, tiled=True),
    )
    token_count = states.shape[0]
    logits = lax.dot_general(table, states, CONTRACT_LAST, preferred_element_type=jnp.float32)
    teach = teacher_logits.astype(jnp.float32)
    vocab_ids = first_row + lax.broadcasted_iota(jnp.int32, logits.shape, 0)
    peak_s, peak_t = lax.pmax(
        (jnp.max(logits, axis=0), jnp.max(teach, axis=0)), ("section", "fsdp")
    )
    student_exp = jnp.exp(logits - peak_s[None, :])
    teach_sum = jnp.sum(jnp.exp(teach - peak_t[None, :]), axis=0)
    sum_s, cross, sum_t = lax.psum(
        (jnp.sum(student_exp, axis=0), jnp.sum(student_exp * (logits - teach), axis=0), teach_sum),
        ("section", "fsdp"),
    )
    log_zs = peak_s + jnp.log(sum_s)
    log_zt = peak_t + jnp.log(sum_t)
    kl_term = cross / sum_s - log_zs + log_zt
    weight = loss_mask.astype(jnp.float32) / token_count
    loss = jnp.sum(weight * kl_term)
    prob = jnp.exp(logits - log_zs[None, :])
    inner = prob * (logits - teach - log_zs[None, :] + log_zt[None, :] - kl_term[None, :])
    grad_logits = (weight[None, :] * inner).astype(jnp.bfloat16)
    selector = (vocab_ids == student_ids[None, :]).astype(jnp.bfloat16)
    table_total = jnp.dot(grad_logits, states, preferred_element_type=jnp.float32)
    table_total = table_total + jnp.dot(selector, cotangent, preferred_element_type=jnp.float32)
    table_grad = table_total.astype(jnp.bfloat16)
    token_part = lax.psum_scatter(
        lax.dot_general(grad_logits, table, CONTRACT_FIRST, preferred_element_type=jnp.float32),
        "fsdp",
        scatter_dimension=0,
        tiled=True,
    )
    state_total = lax.psum_scatter(token_part, "section", scatter_dimension=1, tiled=True)
    return (table_grad, state_total.astype(jnp.bfloat16), loss)


def solution(mesh):
    return jax.shard_map(
        shards,
        mesh=mesh,
        in_specs=(
            P(("section", "fsdp"), None),
            P("fsdp", "section"),
            P("fsdp", "section"),
            P(("section", "fsdp"), None),
            P(),
            P(),
        ),
        out_specs=(P(("section", "fsdp"), None), P("fsdp", "section"), P()),
        check_vma=False,
    )
```

profile of v0, /device:TPU:16, one launch (start us, length us, event | category | flops | bytes accessed | tf_op | source)
XLA Modules:
  0.0 815.7 jit_solution(2197365377452788152)
XLA Ops:
  7.2 0.0 copy-start
  7.2 0.0 reduce-scatter.5.cloned.1.call-start
  7.2 126.4 %all-gather = bf16[32,112,8]{1,2,0:T(8,128)(2,1)S(1)} all-gather(bf16[1,112,8]{1,2,0:T(8,128)(2,1)} %bitcast.25), channel_id=1, replica_groups=mesh['section'=32,'fsdp'=16] {'section'}, dimensions={0}, use_global_device_ids=true | all-gather | bytes 59136 | tf_op jit(solution)/shard_map/all_gather | solution.py:14
  133.6 0.1 reshape.14
  133.7 0.0 copy-start.1
  133.8 0.0 copy-start.4
  133.8 53.0 %all_gather.13 = bf16[128,3584]{1,0:T(8,128)(2,1)S(1)} all-gather(bf16[8,3584]{1,0:T(8,128)(2,1)S(1)} %bitcast.23), channel_id=1, replica_groups=mesh['section'=32,'fsdp'=16] {'fsdp'}, dimensions={0}, use_global_device_ids=true | all-gather | bytes 974848 | tf_op jit(solution)/shard_map/all_gather | solution.py:18
  186.8 0.9 reduce_max.24
  187.7 0.0 copy-done
  187.7 0.6 fusion.7
  188.3 99.3 %all-reduce.1 = (f32[128]{0:T(128)S(1)}, f32[128]{0:T(128)S(1)}) all-reduce(bf16[128]{0:T(256)(128)(2,1)S(1)} %reduce_max.24, f32[128]{0:T(128)S(1)} %get-tuple-element.16), channel_id=1, replica_groups=mesh['section'=32,'fsdp'=16] {'section','fsdp'}, use_global_device_ids=true, to_apply=%region_5.0 | all-reduce | flops 256 | bytes 1792 | tf_op jit(solution)/shard_map/pmax | solution.py:25
  287.6 0.0 copy-done.1
  287.6 0.1 fusion.4
  287.7 100.3 %all-reduce = (f32[128]{0:T(128)S(1)}, f32[128]{0:T(128)S(1)}, f32[128]{0:T(128)S(1)}) all-reduce(f32[128]{0:T(128)S(1)} %get-tuple-element.5, f32[128]{0:T(128)S(1)} %get-tuple-element.4, f32[128]{0:T(128)S(1)} %get-tuple-element.3), channel_id=1, replica_groups=mesh['section'=32,'fsdp'=16] {'section','fsdp'}, use_global_device_ids=true, to_apply=%region_7.0 | all-reduce | flops 384 | bytes 3072 | tf_op jit(solution)/shard_map/psum | solution.py:30
  388.0 0.0 copy-done.4
  388.0 0.6 multiply_reduce_fusion.1
  388.6 0.1 multiply_convert_fusion
  388.7 1.7 fusion.9
  390.3 0.0 copy-start.2
  390.3 0.0 reduce-scatter.5.cloned.1.call-update
  390.3 0.0 reduce-scatter.7.cloned.1.call-start
  390.4 0.6 copy-done.2
  391.0 121.2 %all-gather.1 = bf16[32,112,8]{1,2,0:T(8,128)(2,1)S(1)} all-gather(bf16[1,112,8]{1,2,0:T(8,128)(2,1)S(1)} %bitcast.26), channel_id=1, replica_groups=mesh['section'=32,'fsdp'=16] {'section'}, dimensions={0}, use_global_device_ids=true | all-gather | bytes 59136 | tf_op jit(solution)/shard_map/all_gather | solution.py:15
  512.2 0.1 reshape.16
  512.3 2.4 fusion.8
  514.7 46.2 %all_gather.15 = bf16[128,3584]{1,0:T(8,128)(2,1)S(1)} all-gather(bf16[8,3584]{1,0:T(8,128)(2,1)S(1)} %bitcast.22), channel_id=1, replica_groups=mesh['section'=32,'fsdp'=16] {'fsdp'}, dimensions={0}, use_global_device_ids=true | all-gather | bytes 974848 | tf_op jit(solution)/shard_map/all_gather | solution.py:19
  560.9 2.7 copy.13
  563.6 0.0 reduce-scatter.7.cloned.1.call-update
  563.6 0.0 copy-done.3
  563.6 3.9 fusion
  567.6 239.8 %reduce-scatter.7.cloned.1.call-done = f32[112,8]{1,0:T(8,128)} async-done(((f32[3584,8]{1,0:T(8,128)}), f32[112,8]{1,0:T(8,128)}) %reduce-scatter.7.cloned.1.call-update) | async-done | bytes 3600
  807.4 1.5 copy.14
  (5 shorter events, 0.0 us)
Async XLA Ops:
  7.2 180.5 %copy-start = (bf16[250,3584]{1,0:T(8,128)(2,1)S(1)}, bf16[250,3584]{1,0:T(8,128)(2,1)}, u32[]{:S(2)}) copy-start(bf16[250,3584]{1,0:T(8,128)(2,1)} %param.6) | copy-start | bytes 5376004
  7.2 553.7 %reduce-scatter.5.cloned.1.call-start = ((), (), s32[]{:S(2)}) async-start(), calls=%async_computation.2 | async-start | bytes 1949696 | tf_op jit(solution)/shard_map/reduce_scatter | solution.py:46
  133.7 153.9 %copy-start.1 = (bf16[250,128]{1,0:T(8,128)(2,1)S(1)}, bf16[250,128]{1,0:T(8,128)(2,1)}, u32[]{:S(2)}) copy-start(bf16[250,128]{1,0:T(8,128)(2,1)} %param.9) | copy-start | bytes 192004
  133.8 254.2 %copy-start.4 = (s32[128]{0:T(128)S(1)}, s32[128]{0:T(128)}, u32[]{:S(2)}) copy-start(s32[128]{0:T(128)} %param.11) | copy-start | bytes 1540
  390.3 0.7 copy-start.2
  390.3 417.1 %reduce-scatter.7.cloned.1.call-start = ((), (), s32[]{:S(2)}) async-start(), calls=%async_computation.3 | async-start | bytes 1892352
  560.9 2.7 copy-start.3
Sparse Core Ops, SparseCore 0:
  390.5 111.0 reduce-scatter.4
  563.8 243.6 reduce-scatter.6
where the time goes:
time: 816 us
  blocking collectives  546 us (67%)
  waiting for transfers between devices  240 us (29%)
  between operations  14.1 us (2%)
  matrix products  8.66 us (1%)
    unnamed x3, waiting for transfers between devices  240 us
    all_gather x1, blocking collectives, shards(): lax.all_gather(hidden_states, 'section', axis=1, tiled=True)  126 us
    all_gather x1, blocking collectives, shards(): lax.all_gather(embed_cotangent, 'section', axis=1, tiled=True)  121 us
    psum x1, blocking collectives, shards(): lax.psum((jnp.sum(student_exp, axis=0), jnp.sum(student_exp * (logits - t...  100 us
    pmax x1, blocking collectives, shards(): lax.pmax((jnp.max(logits, axis=0), jnp.max(teach, axis=0)), ('section', '...  99.3 us
    all_gather x1, blocking collectives, shards(): lax.all_gather(columns[0], 'fsdp', axis=0, tiled=True)  53 us
    all_gather x1, blocking collectives, shards(): lax.all_gather(columns[1], 'fsdp', axis=0, tiled=True)  46.2 us
  transfers between devices with their start and end apart: 2, of which 1 were waited for; matrix products, arithmetic and copies ran while one was open for 1% of the time, Pallas kernels for 0%

commit v1 on v0

v1 whole, which is shorter than its diff:
```python
import functools

import jax
import jax.numpy as jnp
from jax import lax
from jax.experimental import pallas as pl
from jax.experimental.pallas import tpu as pltpu
from jax.sharding import PartitionSpec as P

MESH = pl.DeviceIdType.MESH
F32, BF16 = jnp.float32, jnp.bfloat16
CONTRACT_LAST = (((1,), (1,)), ((), ()))
CONTRACT_FIRST = (((0,), (0,)), ((), ()))
NX, NY, NLO, NHI, NCORE = 4, 4, 8, 2, 2
NZ = NLO * NHI
NXY = NX * NY


def merge(maxes, *sums):
    top = jnp.max(maxes, axis=0, keepdims=True)
    scale = jnp.exp(maxes - top)
    return (top, *(jnp.sum(s * scale, axis=0, keepdims=True) for s in sums))


def merge_tiles(ref):
    peak_s, sum_s, cross = merge(ref[:, 0, :], ref[:, 1, :], ref[:, 2, :])
    peak_t, sum_t = merge(ref[:, 3, :], ref[:, 4, :])
    return peak_s, sum_s, cross, peak_t, sum_t


def tile_of(rows):
    return jnp.concatenate([*rows, jnp.zeros((3, rows[0].shape[1]), F32)], axis=0)


def kernel(
    table_hbm, hidden_ref, cot_ref, teach_hbm, ids_ref, mask_ref,
    grad_hbm, state_ref, loss_ref,
    table, teach_in, pack, first, lanes, hc, stat_core, stat_z, stat_xy,
    logits_ref, glog_ref, own_part, out_part, sib_part, t_ref, u_ref, v_ref, w_ref, z_src, z_dst, grad_ref,
    load_sem, store_sem, ag1_send, ag1_recv, ag2_send, ag2_recv, ag3_send, ag3_recv, sib_send, sib_recv,
    st_send, st_recv, rs0_send, rs0_recv, rs1_send, rs1_recv, rs2_send, rs2_recv, rs3_send, rs3_recv,
):
    section, fsdp = lax.axis_index("section"), lax.axis_index("fsdp")
    x, lo = section // NLO, lax.rem(section, NLO)
    y, hi, core = fsdp // (NHI * NCORE), lax.rem(fsdp // NCORE, NHI), lax.rem(fsdp, NCORE)
    z = hi * NLO + lo
    other = 1 - core
    a, b = x + core * (y - x), y + core * (x - y)

    def device(x_, y_, z_, core_):
        return (x_ * NLO + lax.rem(z_, NLO), y_ * (NHI * NCORE) + (z_ // NLO) * NCORE + core_)

    def xy(a_, b_):
        return a_ + core * (b_ - a_), b_ + core * (a_ - b_)

    def send(src, dst, send_sem, recv_sem, target):
        pltpu.make_async_remote_copy(
            src_ref=src, dst_ref=dst, send_sem=send_sem, recv_sem=recv_sem, device_id=target, device_id_type=MESH
        ).start()

    def arrive(ref, sem):
        pltpu.make_async_copy(ref, ref, sem).wait()

    loads = [
        pltpu.make_async_copy(table_hbm, table, load_sem.at[0]),
        pltpu.make_async_copy(teach_hbm, teach_in, load_sem.at[1]),
    ]
    for load in loads:
        load.start()

    barrier = pltpu.get_barrier_semaphore()

    def greet_z(j, carry):
        z_ = lax.rem(z + j, NZ)
        pl.semaphore_signal(barrier, inc=1, device_id=device(x, y, z_, core), device_id_type=MESH)
        pl.semaphore_signal(barrier, inc=1, device_id=device(x, y, z_, other), device_id_type=MESH)
        return carry

    def greet_xy(j, carry):
        p = lax.rem(x * NY + y + j, NXY)
        pl.semaphore_signal(barrier, inc=1, device_id=device(p // NY, lax.rem(p, NY), z, core), device_id_type=MESH)
        return carry

    pl.semaphore_signal(barrier, inc=1, device_id=device(x, y, z, other), device_id_type=MESH)
    lax.fori_loop(1, NZ, greet_z, 0)
    lax.fori_loop(1, NXY, greet_xy, 0)

    pack[...] = jnp.zeros_like(pack)
    pack[:, 0:112] = jnp.concatenate([hidden_ref[...].astype(F32), cot_ref[...].astype(F32)], axis=0).astype(BF16)
    pl.semaphore_wait(barrier, 1 + 2 * (NZ - 1) + NXY - 1)

    def gather_z(j, carry):
        send(pack, first.at[lo, core], ag1_send, ag1_recv, device(x, y, lax.rem(z + j, NZ), hi))
        return carry

    lax.fori_loop(1, NZ, gather_z, 0)

    @pl.when(core == hi)
    def _():
        pltpu.make_async_copy(pack, first.at[lo, core], ag1_recv).start()

    @pl.when(core != hi)
    def _():
        send(pack, first.at[lo, core], ag1_send, ag1_recv, device(x, y, z, hi))

    loads[1].wait()
    teach = teach_in[...].astype(F32)
    top_t = jnp.max(teach, axis=0, keepdims=True)
    total_t = jnp.sum(jnp.exp(teach - top_t), axis=0, keepdims=True)

    arrive(first, ag1_recv)
    for j in range(NLO):
        left, right = first[j, 0].astype(F32), first[j, 1].astype(F32)
        for t in range(2):
            rows = jnp.concatenate([left[8 * t : 8 * t + 8], right[8 * t : 8 * t + 8]], axis=0)
            lanes[t, :, 112 * j : 112 * (j + 1)] = rows[:, 0:112]
    for t in range(2):
        hc[x, t, y, core] = lanes[t].astype(BF16)
        for j in range(1, 4):
            block = hc.at[x, t, y, core]
            send(block, block, ag2_send.at[t], ag2_recv.at[t], device(*xy(a, lax.rem(b + j, 4)), z, core))

    def to_sibling(t, a_):
        for i in range(4):
            xi, yi = xy(a_, i)
            block = hc.at[xi, t, yi, core]
            send(block, block, sib_send.at[t], sib_recv.at[t], device(x, y, z, other))

    def gather_last(t):
        for j in range(1, 4):
            target = device(*xy(lax.rem(a + j, 4), b), z, core)
            for i in range(4):
                xi, yi = xy(a, i)
                block = hc.at[xi, t, yi, core]
                send(block, block, ag3_send.at[t], ag3_recv.at[t], target)

    three = hc.at[0:3, 0, 0, 0]
    twelve = hc.at[0:3, 0, 0:2]
    sixteen = hc.at[0]

    arrive(three, ag2_recv.at[0])
    gather_last(0)
    to_sibling(0, a)
    arrive(three, ag2_recv.at[1])
    to_sibling(1, a)
    loads[0].wait()
    arrive(twelve, ag3_recv.at[0])
    for j in range(1, 4):
        to_sibling(0, lax.rem(a + j, 4))
    gather_last(1)
    arrive(sixteen, sib_recv.at[0])

    total = None
    for c in range(NX):
        states = hc[c, 0].reshape(128, 896)
        term = lax.dot_general(table[:, 896 * c : 896 * (c + 1)], states, CONTRACT_LAST, preferred_element_type=F32)
        total = term if total is None else total + term
    logits_ref[...] = total
    peak = jnp.max(total, axis=0, keepdims=True)
    weights = jnp.exp(total - peak)
    stat_core[core] = tile_of(
        [
            peak,
            jnp.sum(weights, axis=0, keepdims=True),
            jnp.sum(weights * (total - teach), axis=0, keepdims=True),
            top_t,
            total_t,
        ]
    )
    send(stat_core.at[core], stat_core.at[core], st_send.at[0], st_recv.at[0], device(x, y, z, other))
    arrive(stat_core.at[0], st_recv.at[0])
    stat_z[z] = tile_of(merge_tiles(stat_core))

    def share_z(j, carry):
        send(stat_z.at[z], stat_z.at[z], st_send.at[1], st_recv.at[1], device(x, y, lax.rem(z + j, NZ), core))
        return carry

    lax.fori_loop(1, NZ, share_z, 0)
    arrive(twelve, ag3_recv.at[1])
    for j in range(1, 4):
        to_sibling(1, lax.rem(a + j, 4))
    arrive(stat_z.at[0 : NZ - 1], st_recv.at[1])
    me = x * NY + y
    stat_xy[me] = tile_of(merge_tiles(stat_z))

    def share_xy(j, carry):
        p = lax.rem(me + j, NXY)
        send(stat_xy.at[me], stat_xy.at[me], st_send.at[2], st_recv.at[2], device(p // NY, lax.rem(p, NY), z, core))
        return carry

    lax.fori_loop(1, NXY, share_xy, 0)
    arrive(stat_xy.at[0 : NXY - 1], st_recv.at[2])
    peak_s, sum_s, cross, peak_t, sum_t = merge_tiles(stat_xy)

    log_zs = peak_s + jnp.log(sum_s)
    log_zt = peak_t + jnp.log(sum_t)
    kl_term = cross / sum_s - log_zs + log_zt
    weight = mask_ref[...].astype(F32) / 128.0
    loss_ref[...] = jnp.broadcast_to(jnp.sum(weight * kl_term, axis=1, keepdims=True), loss_ref.shape)
    logits = logits_ref[...]
    prob = jnp.exp(logits - log_zs)
    inner = prob * (logits - teach_in[...].astype(F32) - log_zs + log_zt - kl_term)
    glog = (weight * inner).astype(BF16)
    glog_ref[...] = glog

    for c in range(NX):
        part = lax.dot_general(glog, table[:, 896 * c : 896 * (c + 1)], CONTRACT_FIRST, preferred_element_type=F32)
        part = part.reshape(NY, NHI, 16, 896)
        own_part[c] = part
        out_part[c] = part.astype(BF16)
        send(out_part.at[c, :, other], sib_part.at[c], rs0_send.at[c], rs0_recv.at[c], device(x, y, z, other))
    for c in range(NX):
        arrive(sib_part.at[c], rs0_recv.at[c])
        for r in range(NY):
            ai, bi = xy(c, r)
            t_ref[ai, bi] = (own_part[c, r, core] + sib_part[c, r].astype(F32)).astype(BF16)
    for j in range(1, 4):
        a_ = lax.rem(a + j, 4)
        send(t_ref.at[a_], u_ref.at[a], rs1_send, rs1_recv, device(*xy(a_, b), z, core))

    arrive(sixteen, sib_recv.at[1])
    rows = glog_ref.shape[0]
    entries = (section * (NY * NHI * NCORE) + fsdp) * rows + lax.broadcasted_iota(jnp.int32, (rows, 128), 0)
    selector = (entries == ids_ref[...]).astype(BF16)
    both = jnp.concatenate([glog_ref[...], selector], axis=1)
    for c in range(NX):
        grad_ref[:, 896 * c : 896 * (c + 1)] = jnp.dot(
            both, hc[c].reshape(256, 896), preferred_element_type=F32
        ).astype(BF16)
    store = pltpu.make_async_copy(grad_ref, grad_hbm, store_sem)
    store.start()

    arrive(u_ref.at[0:3], rs1_recv)
    for r in range(4):
        acc = t_ref[a, r].astype(F32)
        for j in range(1, 4):
            acc = acc + u_ref[lax.rem(a + j, 4), r].astype(F32)
        v_ref[r] = acc.astype(BF16)
    for j in range(1, 4):
        b_ = lax.rem(b + j, 4)
        send(v_ref.at[b_], w_ref.at[b], rs2_send, rs2_recv, device(*xy(a, b_), z, core))
    arrive(w_ref.at[0:3], rs2_recv)
    acc = v_ref[b].astype(F32)
    for j in range(1, 4):
        acc = acc + w_ref[lax.rem(b + j, 4)].astype(F32)
    lanes[0] = acc
    z_src[...] = jnp.zeros_like(z_src)
    for j in range(NLO):
        for k in range(NCORE):
            z_src[j, k, :, 0:112] = lanes[0, 8 * k : 8 * k + 8, 112 * j : 112 * (j + 1)]

    def reduce_z(j, carry):
        lo_ = lax.rem(lo + j, NLO)
        for k in range(NCORE):
            send(z_src.at[lo_, k], z_dst.at[z], rs3_send, rs3_recv, device(x, y, core * NLO + lo_, k))
        return carry

    lax.fori_loop(1, NLO, reduce_z, 0)
    send(z_src.at[lo, other], z_dst.at[z], rs3_send, rs3_recv, device(x, y, core * NLO + lo, other))

    @pl.when(core == hi)
    def _():
        pltpu.make_async_copy(z_src.at[lo, core], z_dst.at[z], rs3_recv).start()

    @pl.when(core != hi)
    def _():
        send(z_src.at[lo, core], z_dst.at[z], rs3_send, rs3_recv, device(x, y, core * NLO + lo, core))

    arrive(z_dst, rs3_recv)
    state_ref[...] = jnp.sum(z_dst[...], axis=0)[:, 0:112].astype(BF16)

    tiles = first.reshape(NZ, 16, 128)

    @pl.when(core == hi)
    def _():
        arrive(tiles.at[0 : NZ - 1], ag1_send)
        arrive(z_dst.at[0 : NZ - 1], rs3_send)

    @pl.when(core != hi)
    def _():
        arrive(tiles, ag1_send)
        arrive(z_dst, rs3_send)

    for t in range(2):
        arrive(three, ag2_send.at[t])
        arrive(twelve, ag3_send.at[t])
        arrive(sixteen, sib_send.at[t])
    arrive(stat_core.at[0], st_send.at[0])
    arrive(stat_z.at[0 : NZ - 1], st_send.at[1])
    arrive(stat_xy.at[0 : NXY - 1], st_send.at[2])
    for c in range(NX):
        arrive(sib_part.at[c], rs0_send.at[c])
    arrive(u_ref.at[0:3], rs1_send)
    arrive(w_ref.at[0:3], rs2_send)
    store.wait()


def shards(table, hidden_states, embed_cotangent, teacher_logits, student_ids, loss_mask):
    rows, width = table.shape
    tokens = teacher_logits.shape[1]
    vmem = pl.BlockSpec(memory_space=pltpu.VMEM)
    hbm = pl.BlockSpec(memory_space=pl.ANY)
    dma = pltpu.SemaphoreType.DMA
    table_grad, state_grad, loss = pl.pallas_call(
        kernel,
        out_shape=(
            jax.ShapeDtypeStruct((rows, width), BF16),
            jax.ShapeDtypeStruct(hidden_states.shape, BF16),
            jax.ShapeDtypeStruct((1, 128), F32),
        ),
        in_specs=[hbm, vmem, vmem, hbm, vmem, vmem],
        out_specs=(hbm, vmem, vmem),
        scratch_shapes=[
            pltpu.VMEM((rows, width), BF16),
            pltpu.VMEM((rows, tokens), BF16),
            pltpu.VMEM((16, 128), BF16),
            pltpu.VMEM((NLO, NCORE, 16, 128), BF16),
            pltpu.VMEM((2, 16, 896), F32),
            pltpu.VMEM((NX, 2, NY, NHI, 16, 896), BF16),
            pltpu.VMEM((NCORE, 8, 128), F32),
            pltpu.VMEM((NZ, 8, 128), F32),
            pltpu.VMEM((NXY, 8, 128), F32),
            pltpu.VMEM((rows, tokens), F32),
            pltpu.VMEM((rows, tokens), BF16),
            pltpu.VMEM((NX, NY, NHI, 16, 896), F32),
            pltpu.VMEM((NX, NY, NHI, 16, 896), BF16),
            pltpu.VMEM((NX, NY, 16, 896), BF16),
            pltpu.VMEM((4, 4, 16, 896), BF16),
            pltpu.VMEM((4, 4, 16, 896), BF16),
            pltpu.VMEM((4, 16, 896), BF16),
            pltpu.VMEM((4, 16, 896), BF16),
            pltpu.VMEM((NLO, NCORE, 8, 128), F32),
            pltpu.VMEM((NZ, 8, 128), F32),
            pltpu.VMEM((rows, width), BF16),
            dma((2,)),
            dma,
            dma,
            dma,
            dma((2,)),
            dma((2,)),
            dma((2,)),
            dma((2,)),
            dma((2,)),
            dma((2,)),
            dma((3,)),
            dma((3,)),
            dma((4,)),
            dma((4,)),
            dma,
            dma,
            dma,
            dma,
            dma,
            dma,
        ],
        compiler_params=pltpu.CompilerParams(
            collective_id=0, has_side_effects=True, vmem_limit_bytes=40 * 1024 * 1024
        ),
    )(
        table,
        hidden_states,
        embed_cotangent,
        teacher_logits,
        student_ids.reshape(1, 128),
        loss_mask.reshape(1, 128),
    )
    return table_grad, state_grad, loss[0, 0]


def solution(mesh):
    return jax.shard_map(
        shards,
        mesh=mesh,
        in_specs=(
            P(("section", "fsdp"), None),
            P("fsdp", "section"),
            P("fsdp", "section"),
            P(("section", "fsdp"), None),
            P(),
            P(),
        ),
        out_specs=(P(("section", "fsdp"), None), P("fsdp", "section"), P()),
        check_vma=False,
    )
```

time: 816 us -> 79 us (0.10)
  the two profiles are of different devices: /device:TPU:16 before, /device:TPU:1 now
where the time goes in v1:
time: 79 us; the launch traced here: 78.7 us
  Pallas kernels  70.1 us (89%)
  local copies, waits for them, and re-layouts  6.81 us (9%)
  between operations  1.82 us (2%)
    pallas_call x1, Pallas kernels, shards(): pl.pallas_call(kernel, out_shape=(jax.ShapeDtypeStruct((rows, width), BF1...  70.1 us
    unnamed x14, local copies, waits for them, and re-layouts  6.81 us

profile of v1, /device:TPU:1, one launch (start us, length us, event | category | flops | bytes accessed | tf_op | source)
XLA Modules:
  0.0 78.7 jit_solution(14302013271573882650)
XLA Ops:
  0.6 0.0 copy-start
  0.6 1.5 %copy-done = bf16[250,3584]{1,0:T(8,128)(2,1)S(1)} copy-done((bf16[250,3584]{1,0:T(8,128)(2,1)S(1)}, bf16[250,3584]{1,0:T(8,128)(2,1)}, u32[]{:S(2)}) %copy-start) | copy-done | bytes 1792024
  2.1 0.0 copy-start.1
  2.1 0.8 %copy-done.1 = bf16[250,128]{1,0:T(8,128)(2,1)S(1)} copy-done((bf16[250,128]{1,0:T(8,128)(2,1)S(1)}, bf16[250,128]{1,0:T(8,128)(2,1)}, u32[]{:S(2)}) %copy-start.1) | copy-done | bytes 64024
  3.0 0.0 copy-start.2
  3.0 0.7 copy-done.2
  3.7 0.0 copy-start.3
  3.7 0.7 copy-done.3
  4.3 0.0 copy-start.4
  4.3 0.7 copy-done.4
  5.0 0.0 copy-start.5
  5.0 0.7 copy-done.5
  5.6 70.1 %shard_map.85 = (bf16[250,3584]{1,0:T(8,128)(2,1)S(1)}, bf16[8,112]{1,0:T(8,128)(2,1)S(1)}, f32[1,128]{1,0:T(1,128)S(1)}) custom-call(bf16[250,3584]{1,0:T(8,128)(2,1)S(1)} %copy-done, bf16[8,112]{1,0:T(8,128)(2,1)S(1)} %copy-done.2, bf16[8,112]{1,0:T(8,128)(2,1)S(1)} %copy-done.3, bf16[250,128]{1,0:T(8,128)(2,1)S(1)} %copy-done.1, s32[1,128]{1,0:T(1,128)S(1)} %bitcast.4, ...), custom_call_target="tpu_custom_call" | custom-call | tf_op jit(solution)/shard_map/pallas_call | solution.py:304
  75.7 1.2 %copy.12 = bf16[250,3584]{1,0:T(8,128)(2,1)} copy(bf16[250,3584]{1,0:T(8,128)(2,1)S(1)} %get-tuple-element.12) | data formatting | bytes 3584000
  76.9 0.6 copy.13
Async XLA Ops:
  0.6 1.5 %copy-start = (bf16[250,3584]{1,0:T(8,128)(2,1)S(1)}, bf16[250,3584]{1,0:T(8,128)(2,1)}, u32[]{:S(2)}) copy-start(bf16[250,3584]{1,0:T(8,128)(2,1)} %table_hbm.1) | copy-start | bytes 5376004
  2.1 0.8 %copy-start.1 = (bf16[250,128]{1,0:T(8,128)(2,1)S(1)}, bf16[250,128]{1,0:T(8,128)(2,1)}, u32[]{:S(2)}) copy-start(bf16[250,128]{1,0:T(8,128)(2,1)} %teach_hbm.1) | copy-start | bytes 192004
  3.0 0.7 copy-start.2
  3.7 0.7 copy-start.3
  4.3 0.7 copy-start.4
  5.0 0.7 copy-start.5

commit v2 on v0

v2 whole, which is shorter than its diff:
```python
import functools

import jax
import jax.numpy as jnp
from jax import lax
from jax.experimental import pallas as pl
from jax.experimental.pallas import tpu as pltpu
from jax.sharding import PartitionSpec as P

MESH = pl.DeviceIdType.MESH
F32, BF16 = jnp.float32, jnp.bfloat16
CONTRACT_LAST = (((1,), (1,)), ((), ()))
CONTRACT_FIRST = (((0,), (0,)), ((), ()))
NX, NY, NLO, NHI, NCORE = 4, 4, 8, 2, 2
NZ = NLO * NHI
NXY = NX * NY
VMEM_MIB = 60
FAR_Z = sorted(range(1, NZ), key=lambda j: -min(j, NZ - j))
FAR_XY = sorted(
    ((i, j) for i in range(NX) for j in range(NY) if i or j), key=lambda d: -sum(min(v, 4 - v) for v in d)
)


def merge(maxes, *sums):
    top = jnp.max(maxes, axis=0, keepdims=True)
    scale = jnp.exp(maxes - top)
    return (top, *(jnp.sum(s * scale, axis=0, keepdims=True) for s in sums))


def merge_tiles(ref):
    peak_s, sum_s, cross = merge(ref[:, 0, :], ref[:, 1, :], ref[:, 2, :])
    peak_t, sum_t = merge(ref[:, 3, :], ref[:, 4, :])
    return peak_s, sum_s, cross, peak_t, sum_t


def tile_of(rows):
    return jnp.concatenate([*rows, jnp.zeros((3, rows[0].shape[1]), F32)], axis=0)


class Copies:
    def __init__(self):
        self.arrivals, self.departures = {}, {}

    @staticmethod
    def wait(ref, sem):
        pltpu.make_async_copy(ref, ref, sem).wait()

    @staticmethod
    def send(src, dst, sems, target):
        pltpu.make_async_remote_copy(
            src_ref=src, dst_ref=dst, send_sem=sems[0], recv_sem=sems[1], device_id=target, device_id_type=MESH
        ).start()

    def expect(self, key, ref, sems):
        self.arrivals[key] = (ref, sems[1])
        self.departures[key] = (ref, sems[0])

    def arrive(self, key):
        self.wait(*self.arrivals.pop(key))

    def finish(self):
        for key in list(self.arrivals):
            self.arrive(key)
        for ref, sem in self.departures.values():
            self.wait(ref, sem)


def kernel(
    table_hbm, hidden_hbm, cot_hbm, teach_hbm, ids_hbm, mask_hbm,
    grad_hbm, state_ref, loss_ref,
    table, hidden_in, cot_in, teach_in, ids_in, mask_in,
    pack, first, lanes, hc, stat_core, stat_xy, stat_z,
    logits_ref, part, sib_part, t_ref, u_ref, cols_ref, z_src, z_dst, grad_ref,
    load_sem, store_sem, ag1_sem, plane_send, plane_recv, sib_sem, st_sem, rs0_sem, rs1_sem, rs2_sem,
):
    section, fsdp = lax.axis_index("section"), lax.axis_index("fsdp")
    x, lo = section // NLO, lax.rem(section, NLO)
    y, hi, core = fsdp // (NHI * NCORE), lax.rem(fsdp // NCORE, NHI), lax.rem(fsdp, NCORE)
    z, me = hi * NLO + lo, x * NY + y
    other = 1 - core

    def device(x_, y_, z_, core_):
        return (x_ * NLO + lax.rem(z_, NLO), y_ * (NHI * NCORE) + (z_ // NLO) * NCORE + core_)

    sibling = device(x, y, z, other)
    along_z = [lax.rem(z + j, NZ) for j in FAR_Z]
    in_plane = [(lax.rem(x + i, NX), lax.rem(y + j, NY)) for i, j in FAR_XY]
    copies = Copies()
    send = copies.send

    def pair(ref, *at):
        return ref.at[(0, *at)], ref.at[(1, *at)]

    loads = [
        pltpu.make_async_copy(src, dst, load_sem.at[i])
        for i, (src, dst) in enumerate(
            [
                (hidden_hbm, hidden_in), (cot_hbm, cot_in), (teach_hbm, teach_in),
                (table_hbm, table), (ids_hbm, ids_in), (mask_hbm, mask_in),
            ]
        )
    ]
    loads[0].start()
    loads[1].start()

    barrier = pltpu.get_barrier_semaphore()
    for z_ in along_z:
        pl.semaphore_signal(barrier, inc=1, device_id=device(x, y, z_, core), device_id_type=MESH)
        pl.semaphore_signal(barrier, inc=1, device_id=device(x, y, z_, other), device_id_type=MESH)
    for x_, y_ in in_plane:
        pl.semaphore_signal(barrier, inc=1, device_id=device(x_, y_, z, core), device_id_type=MESH)
    pl.semaphore_signal(barrier, inc=1, device_id=sibling, device_id_type=MESH)
    for load in loads[2:]:
        load.start()

    loads[0].wait()
    loads[1].wait()
    pack[...] = jnp.zeros_like(pack)
    pack[:, 0:112] = jnp.concatenate([hidden_in[...].astype(F32), cot_in[...].astype(F32)], axis=0).astype(BF16)
    pl.semaphore_wait(barrier, 1 + 2 * (NZ - 1) + NXY - 1)

    waited = [0, 1]
    tiles = first.reshape(NZ, 16, 128)
    gathers, stores = [], []

    def finish():
        for i, load in enumerate(loads):
            if i not in waited:
                load.wait()
        for sem, ref, less in gathers:

            @pl.when(core == hi)
            def _():
                copies.wait(less, sem)

            @pl.when(core != hi)
            def _():
                copies.wait(ref, sem)

        copies.finish()
        for store in stores:
            store.wait()


    sems = pair(ag1_sem)
    for z_ in along_z:
        send(pack, first.at[lo, core], sems, device(x, y, z_, hi))

    @pl.when(core == hi)
    def _():
        pltpu.make_async_copy(pack, first.at[lo, core], sems[1]).start()

    @pl.when(core != hi)
    def _():
        send(pack, first.at[lo, core], sems, device(x, y, z, hi))

    copies.arrivals["first"] = (first, sems[1])
    gathers.append((sems[0], tiles, tiles.at[0 : NZ - 1]))

    loads[2].wait()
    waited.append(2)
    teach = teach_in[...].astype(F32)
    top_t = jnp.max(teach, axis=0, keepdims=True)
    total_t = jnp.sum(jnp.exp(teach - top_t), axis=0, keepdims=True)

    copies.arrive("first")

    sib_sems = [pair(sib_sem, t) for t in range(2)]
    for t in range(2):
        for j in range(NLO):
            left, right = first[j, 0].astype(F32), first[j, 1].astype(F32)
            rows = jnp.concatenate([left[8 * t : 8 * t + 8], right[8 * t : 8 * t + 8]], axis=0)
            lanes[t, :, 112 * j : 112 * (j + 1)] = rows[:, 0:112]
        block = hc.at[x, t, y, core]
        block[...] = lanes[t].astype(BF16)
        for x_, y_ in in_plane:
            send(block, block, (plane_send.at[t], plane_recv.at[t, me]), device(x_, y_, z, core))
        copies.departures[("plane", t)] = (hc.at[0:3, t, 0:4, 0], plane_send.at[t])
        send(block, block, sib_sems[t], sibling)
        copies.departures[("plane3", t)] = (hc.at[0:3, t, 0, 0], plane_send.at[t])
        for n, (x_, y_) in enumerate(in_plane):
            copies.arrivals[("plane", t, n)] = (hc.at[x_, t, y_, core], plane_recv.at[t, x_ * NY + y_])

    def to_sibling(t):
        for n, (x_, y_) in list(enumerate(in_plane))[::-1]:
            copies.arrive(("plane", t, n))
            block = hc.at[x_, t, y_, core]
            send(block, block, sib_sems[t], sibling)
        copies.expect(("sib", t), hc.at[0], sib_sems[t])

    copies.expect(("sib", 0), hc.at[0, 0, 0, 0], sib_sems[0])
    copies.expect(("sib", 1), hc.at[0, 0, 0, 0], sib_sems[1])
    to_sibling(0)
    copies.arrive(("sib", 0))

    loads[3].wait()
    waited.append(3)
    total = None
    for c in range(NX):
        states = hc[c, 0].reshape(128, 896)
        term = lax.dot_general(table[:, 896 * c : 896 * (c + 1)], states, CONTRACT_LAST, preferred_element_type=F32)
        total = term if total is None else total + term
    logits_ref[...] = total
    peak = jnp.max(total, axis=0, keepdims=True)
    weights = jnp.exp(total - peak)
    gap = total - teach
    stat_core[core] = tile_of(
        [peak, jnp.sum(weights, axis=0, keepdims=True), jnp.sum(weights * gap, axis=0, keepdims=True), top_t, total_t]
    )
    sems = pair(st_sem, 0)
    send(stat_core.at[core], stat_core.at[core], sems, sibling)
    copies.expect("st0", stat_core.at[0], sems)
    copies.arrive("st0")
    chip = merge_tiles(stat_core)
    stat_xy[me] = tile_of(chip)
    sems = pair(st_sem, 1)
    for x_, y_ in in_plane:
        send(stat_xy.at[me], stat_xy.at[me], sems, device(x_, y_, z, core))
    copies.expect("st1", stat_xy.at[0 : NXY - 1], sems)

    p = jnp.exp(total - chip[0])
    both = jnp.concatenate([(p * (gap - chip[2] / chip[1])).astype(BF16), p.astype(BF16)], axis=1)
    order = [lax.rem(x + i, NX) for i in (2, 1, 3, 0)]
    for i, c in enumerate(order):
        columns = table[:, pl.ds(pl.multiple_of(896 * c, 128), 896)]
        sums = lax.dot_general(both, columns, CONTRACT_FIRST, preferred_element_type=F32)
        part[i] = sums.astype(BF16).reshape(2, NY, NHI, 16, 896)
        sems = pair(rs0_sem, i)
        send(part.at[i, :, :, other], sib_part.at[i], sems, sibling)
        copies.expect(("rs0", i), sib_part.at[i], sems)
    sems = pair(rs1_sem)
    for i, c in enumerate(order):
        copies.arrive(("rs0", i))
        for r in range(NY):
            for k in range(2):
                t_ref[i, r, k] = (part[i, k, r, core].astype(F32) + sib_part[i, k, r].astype(F32)).astype(BF16)
        for j in (2, 1, 3, 0):
            y_ = lax.rem(y + j, NY)
            if i < 3 or j > 0:
                send(t_ref.at[i, y_], u_ref.at[me], sems, device(c, y_, z, core))
            else:
                u_ref[me] = t_ref[i, y_]
    copies.expect("rs1", u_ref.at[0 : NXY - 1], sems)

    copies.arrive("st1")
    stat_z[z] = tile_of(merge_tiles(stat_xy))
    sems = pair(st_sem, 2)
    for z_ in along_z:
        send(stat_z.at[z], stat_z.at[z], sems, device(x, y, z_, core))
    copies.expect("st2", stat_z.at[0 : NZ - 1], sems)
    to_sibling(1)
    copies.arrive("st2")
    peak_s, sum_s, cross, peak_t, sum_t = merge_tiles(stat_z)

    loads[4].wait()
    loads[5].wait()
    waited.extend([4, 5])
    log_zs = peak_s + jnp.log(sum_s)
    log_zt = peak_t + jnp.log(sum_t)
    kl_term = cross / sum_s - log_zs + log_zt
    weight = mask_in[...].astype(F32) / 128.0
    loss_ref[...] = jnp.broadcast_to(jnp.sum(weight * kl_term, axis=1, keepdims=True), loss_ref.shape)
    scale = weight / sum_s * jnp.exp(stat_xy[:, 0, :] - peak_s)
    shift = scale * (stat_xy[:, 2, :] / stat_xy[:, 1, :] - cross / sum_s)
    cols_ref[...] = jnp.concatenate([scale, shift, jnp.zeros((128 - 2 * NXY, 128), F32)], axis=0).T
    cols = cols_ref[pl.ds(pl.multiple_of(y * 32 + core * 16, 16), 16), :]

    copies.arrive("rs1")
    acc = jnp.zeros((16, 896), F32)
    for j in range(NXY):
        acc = acc + cols[:, j : j + 1] * u_ref[j, 0].astype(F32)
        acc = acc + cols[:, NXY + j : NXY + j + 1] * u_ref[j, 1].astype(F32)
    lanes[0] = acc
    z_src[...] = jnp.zeros_like(z_src)
    for j in range(NLO):
        for k in range(NCORE):
            z_src[j, k, :, 0:112] = lanes[0, 8 * k : 8 * k + 8, 112 * j : 112 * (j + 1)]

    sems = pair(rs2_sem)
    for j in (0, 7, 1, 6, 2, 5, 3, 4):
        lo_ = lax.rem(lo + j, NLO)
        send(z_src.at[lo_, other], z_dst.at[z], sems, device(x, y, core * NLO + lo_, other))
        if j > 0:
            send(z_src.at[lo_, core], z_dst.at[z], sems, device(x, y, core * NLO + lo_, core))
        else:

            @pl.when(core == hi)
            def _():
                pltpu.make_async_copy(z_src.at[lo, core], z_dst.at[z], sems[1]).start()

            @pl.when(core != hi)
            def _():
                send(z_src.at[lo, core], z_dst.at[z], sems, device(x, y, core * NLO + lo, core))

    copies.arrivals["rs2"] = (z_dst, sems[1])
    gathers.append((sems[0], z_dst, z_dst.at[0 : NZ - 1]))

    copies.arrive(("sib", 1))
    logits = logits_ref[...]
    prob = jnp.exp(logits - log_zs)
    inner = prob * (logits - teach_in[...].astype(F32) - log_zs + log_zt - kl_term)
    glog = (weight * inner).astype(BF16)
    rows = glog.shape[0]
    entries = (section * (NY * NHI * NCORE) + fsdp) * rows + lax.broadcasted_iota(jnp.int32, (rows, 128), 0)
    selector = (entries == ids_in[...]).astype(BF16)
    both = jnp.concatenate([glog, selector], axis=1)
    for c in range(NX):
        grad_ref[:, 896 * c : 896 * (c + 1)] = jnp.dot(
            both, hc[c].reshape(256, 896), preferred_element_type=F32
        ).astype(BF16)
    store = pltpu.make_async_copy(grad_ref, grad_hbm, store_sem)
    store.start()
    stores.append(store)
    copies.arrive("rs2")
    state_ref[...] = jnp.sum(z_dst[...], axis=0)[:, 0:112].astype(BF16)
    finish()


def shards(table, hidden_states, embed_cotangent, teacher_logits, student_ids, loss_mask):
    rows, width = table.shape
    tokens = teacher_logits.shape[1]
    block = hidden_states.shape
    vmem = pl.BlockSpec(memory_space=pltpu.VMEM)
    hbm = pl.BlockSpec(memory_space=pltpu.HBM)
    dma = pltpu.SemaphoreType.DMA
    table_grad, state_grad, loss = pl.pallas_call(
        kernel,
        out_shape=(
            jax.ShapeDtypeStruct((rows, width), BF16),
            jax.ShapeDtypeStruct(block, BF16),
            jax.ShapeDtypeStruct((1, 128), F32),
        ),
        in_specs=[hbm] * 6,
        out_specs=(pl.BlockSpec(memory_space=pl.ANY), vmem, vmem),
        scratch_shapes=[
            pltpu.VMEM((rows, width), BF16),
            pltpu.VMEM(block, BF16),
            pltpu.VMEM(block, BF16),
            pltpu.VMEM((rows, tokens), BF16),
            pltpu.VMEM((1, 128), jnp.int32),
            pltpu.VMEM((1, 128), jnp.int32),
            pltpu.VMEM((16, 128), BF16),
            pltpu.VMEM((NLO, NCORE, 16, 128), BF16),
            pltpu.VMEM((2, 16, 896), F32),
            pltpu.VMEM((NX, 2, NY, NHI, 16, 896), BF16),
            pltpu.VMEM((NCORE, 8, 128), F32),
            pltpu.VMEM((NXY, 8, 128), F32),
            pltpu.VMEM((NZ, 8, 128), F32),
            pltpu.VMEM((rows, tokens), F32),
            pltpu.VMEM((NX, 2, NY, NHI, 16, 896), BF16),
            pltpu.VMEM((NX, 2, NY, 16, 896), BF16),
            pltpu.VMEM((NX, NY, 2, 16, 896), BF16),
            pltpu.VMEM((NXY, 2, 16, 896), BF16),
            pltpu.VMEM((128, 128), F32),
            pltpu.VMEM((NLO, NCORE, 8, 128), F32),
            pltpu.VMEM((NZ, 8, 128), F32),
            pltpu.VMEM((rows, width), BF16),
            dma((6,)),
            dma,
            dma((2,)),
            dma((2,)),
            dma((2, NXY)),
            dma((2, 2)),
            dma((2, 3)),
            dma((2, NX)),
            dma((2,)),
            dma((2,)),
        ],
        compiler_params=pltpu.CompilerParams(
            collective_id=0, has_side_effects=True, vmem_limit_bytes=VMEM_MIB * 1024 * 1024
        ),
    )(
        table,
        hidden_states,
        embed_cotangent,
        teacher_logits,
        student_ids.reshape(1, 128),
        loss_mask.reshape(1, 128),
    )
    return table_grad, state_grad, loss[0, 0]


def solution(mesh):
    return jax.shard_map(
        shards,
        mesh=mesh,
        in_specs=(
            P(("section", "fsdp"), None),
            P("fsdp", "section"),
            P("fsdp", "section"),
            P(("section", "fsdp"), None),
            P(),
            P(),
        ),
        out_specs=(P(("section", "fsdp"), None), P("fsdp", "section"), P()),
        check_vma=False,
    )
```

time: 816 us -> 65.9 us (0.08)
  the two profiles are of different devices: /device:TPU:16 before, /device:TPU:1 now
where the time goes in v2:
time: 65.9 us; the launch traced here: 65.8 us
  Pallas kernels  60.5 us (92%)
  local copies, waits for them, and re-layouts  3.43 us (5%)
  between operations  1.82 us (3%)
    pallas_call x1, Pallas kernels, shards(): pl.pallas_call(kernel, out_shape=(jax.ShapeDtypeStruct((rows, width), BF1...  60.5 us
    unnamed x6, local copies, waits for them, and re-layouts  3.43 us

profile of v2, /device:TPU:1, one launch (start us, length us, event | category | flops | bytes accessed | tf_op | source)
XLA Modules:
  0.0 65.8 jit_solution(10371956071640312590)
XLA Ops:
  0.6 60.5 %shard_map.85 = (bf16[250,3584]{1,0:T(8,128)(2,1)}, bf16[8,112]{1,0:T(8,128)(2,1)}, f32[1,128]{1,0:T(1,128)}) custom-call(bf16[250,3584]{1,0:T(8,128)(2,1)} %table_hbm.1, bf16[8,112]{1,0:T(8,128)(2,1)} %hidden_hbm.1, bf16[8,112]{1,0:T(8,128)(2,1)} %cot_hbm.1, bf16[250,128]{1,0:T(8,128)(2,1)} %teach_hbm.1, s32[1,128]{1,0:T(1,128)} %bitcast.4, s32[1,128]{1,0:T(1,128)} %bitcast.5), custom_call_target="tpu_custom_call" | custom-call | tf_op jit(solution)/shard_map/pallas_call | solution.py:326
  61.1 0.0 copy-start
  61.1 0.0 copy-start.1
  61.2 2.8 %copy.12 = bf16[250,3584]{1,0:T(8,128)(2,1)} copy(bf16[250,3584]{1,0:T(8,128)(2,1)} %get-tuple-element.12) | data formatting | bytes 3584000
  64.0 0.0 copy-done
  64.0 0.6 copy.13
  64.6 0.0 copy-done.1
Async XLA Ops:
  61.1 2.9 %copy-start = (bf16[8,112]{1,0:T(8,128)(2,1)S(1)}, bf16[8,112]{1,0:T(8,128)(2,1)}, u32[]{:S(2)}) copy-start(bf16[8,112]{1,0:T(8,128)(2,1)} %get-tuple-element.13) | copy-start | bytes 5380
  61.1 3.4 %copy-start.1 = (f32[1,128]{1,0:T(1,128)S(1)}, f32[1,128]{1,0:T(1,128)}, u32[]{:S(2)}) copy-start(f32[1,128]{1,0:T(1,128)} %get-tuple-element.8) | copy-start | bytes 1540

commit v3 on v2

v3 whole, which is shorter than its diff:
```python
import functools

import jax
import jax.numpy as jnp
from jax import lax
from jax.experimental import pallas as pl
from jax.experimental.pallas import tpu as pltpu
from jax.sharding import PartitionSpec as P

MESH = pl.DeviceIdType.MESH
F32, BF16 = jnp.float32, jnp.bfloat16
CONTRACT_LAST = (((1,), (1,)), ((), ()))
CONTRACT_FIRST = (((0,), (0,)), ((), ()))
NX, NY, NLO, NHI, NCORE = 4, 4, 8, 2, 2
NZ = NLO * NHI
NXY = NX * NY
VMEM_MIB = 60
FAR_Z = sorted(range(1, NZ), key=lambda j: -min(j, NZ - j))
FAR_XY = sorted(
    ((i, j) for i in range(NX) for j in range(NY) if i or j), key=lambda d: -sum(min(v, 4 - v) for v in d)
)


def merge(maxes, *sums):
    top = jnp.max(maxes, axis=0, keepdims=True)
    scale = jnp.exp(maxes - top)
    return (top, *(jnp.sum(s * scale, axis=0, keepdims=True) for s in sums))


def merge_tiles(ref):
    peak_s, sum_s, cross = merge(ref[:, 0, :], ref[:, 1, :], ref[:, 2, :])
    peak_t, sum_t = merge(ref[:, 3, :], ref[:, 4, :])
    return peak_s, sum_s, cross, peak_t, sum_t


def tile_of(rows):
    return jnp.concatenate([*rows, jnp.zeros((3, rows[0].shape[1]), F32)], axis=0)


class Copies:
    def __init__(self):
        self.arrivals, self.departures = {}, {}

    @staticmethod
    def wait(ref, sem):
        pltpu.make_async_copy(ref, ref, sem).wait()

    @staticmethod
    def send(src, dst, sems, target):
        pltpu.make_async_remote_copy(
            src_ref=src, dst_ref=dst, send_sem=sems[0], recv_sem=sems[1], device_id=target, device_id_type=MESH
        ).start()

    def expect(self, key, ref, sems):
        self.arrivals[key] = (ref, sems[1])
        self.departures[key] = (ref, sems[0])

    def arrive(self, key):
        self.wait(*self.arrivals.pop(key))

    def finish(self):
        for key in list(self.arrivals):
            self.arrive(key)
        for ref, sem in self.departures.values():
            self.wait(ref, sem)


def kernel(
    table_hbm, hidden_hbm, cot_hbm, teach_hbm, ids_hbm, mask_hbm,
    grad_hbm, state_ref, loss_ref,
    table, hidden_in, cot_in, teach_in, ids_in, mask_in,
    pack, first, lanes, hc, stat_xy, stat_z, teach_ref, logits_ref,
    t_ref, u_ref, cols_ref, z_src, z_dst, g_out, g_all, loss_x, grad_ref,
    load_sem, store_sem, ag1_sem, pre_sem, plane_send, plane_recv, sib_sem, st_sem, rs1_sem, rs2_sem, g_sem,
):
    section, fsdp = lax.axis_index("section"), lax.axis_index("fsdp")
    x, lo = section // NLO, lax.rem(section, NLO)
    y, hi, core = fsdp // (NHI * NCORE), lax.rem(fsdp // NCORE, NHI), lax.rem(fsdp, NCORE)
    z, me = hi * NLO + lo, x * NY + y
    other = 1 - core

    def device(x_, y_, z_, core_):
        return (x_ * NLO + lax.rem(z_, NLO), y_ * (NHI * NCORE) + (z_ // NLO) * NCORE + core_)

    sibling = device(x, y, z, other)
    along_z = [lax.rem(z + j, NZ) for j in FAR_Z]
    in_plane = [(lax.rem(x + i, NX), lax.rem(y + j, NY)) for i, j in FAR_XY]
    copies = Copies()
    send = copies.send

    def pair(ref, *at):
        return ref.at[(0, *at)], ref.at[(1, *at)]

    def own_half(v):
        halves = [
            jnp.concatenate([v[:, 32 * q + 16 * h : 32 * q + 16 * h + 16] for q in range(NY)] * 2, axis=1)
            for h in range(2)
        ]
        return jnp.where(core == 0, halves[0], halves[1])

    def left_lanes(shape):
        return lax.broadcasted_iota(jnp.int32, shape, 1) < 64

    loads = [
        pltpu.make_async_copy(src, dst, load_sem.at[i])
        for i, (src, dst) in enumerate(
            [
                (hidden_hbm, hidden_in), (cot_hbm, cot_in), (teach_hbm, teach_in.at[core]),
                (table_hbm, table.at[core]), (ids_hbm, ids_in), (mask_hbm, mask_in),
            ]
        )
    ]
    loads[0].start()
    loads[1].start()

    barrier = pltpu.get_barrier_semaphore()
    for z_ in along_z:
        pl.semaphore_signal(barrier, inc=1, device_id=device(x, y, z_, core), device_id_type=MESH)
        pl.semaphore_signal(barrier, inc=1, device_id=device(x, y, z_, other), device_id_type=MESH)
    for x_, y_ in in_plane:
        pl.semaphore_signal(barrier, inc=1, device_id=device(x_, y_, z, core), device_id_type=MESH)
    pl.semaphore_signal(barrier, inc=1, device_id=sibling, device_id_type=MESH)
    for load in loads[2:]:
        load.start()

    loads[0].wait()
    loads[1].wait()
    pack[...] = jnp.zeros_like(pack)
    pack[:, 0:112] = jnp.concatenate([hidden_in[...].astype(F32), cot_in[...].astype(F32)], axis=0).astype(BF16)
    pl.semaphore_wait(barrier, 1 + 2 * (NZ - 1) + NXY - 1)

    sems = pair(ag1_sem)
    for z_ in along_z:
        send(pack, first.at[lo, core], sems, device(x, y, z_, hi))

    @pl.when(core == hi)
    def _():
        pltpu.make_async_copy(pack, first.at[lo, core], sems[1]).start()

    @pl.when(core != hi)
    def _():
        send(pack, first.at[lo, core], sems, device(x, y, z, hi))

    for i, (src, dst) in enumerate(((teach_hbm, teach_in), (table_hbm, table))):
        sems = pair(pre_sem, i)
        send(src, dst.at[core], sems, sibling)
        copies.expect(("pre", i), dst.at[0], sems)
    for load in loads[2:]:
        load.wait()
    copies.arrive(("pre", 0))
    for s in range(2):
        teach_ref[s] = own_half(teach_in[s].astype(F32))
    top_t = jnp.max(jnp.maximum(teach_ref[0], teach_ref[1]), axis=0, keepdims=True)
    total_t = jnp.sum(jnp.exp(teach_ref[0] - top_t) + jnp.exp(teach_ref[1] - top_t), axis=0, keepdims=True)
    weight = own_half(mask_in[...].astype(F32) / 128.0)

    copies.wait(first, ag1_sem.at[1])

    def share(t):
        block = hc.at[x, t, core, y]
        for x_, y_ in in_plane:
            send(block, block, (plane_send.at[t], plane_recv.at[t, me]), device(x_, y_, z, core))

    def gathered(t):
        for x_, y_ in in_plane[::-1]:
            copies.wait(hc.at[x_, t, core, y_], plane_recv.at[t, x_ * NY + y_])

    def to_sibling(t):
        half = hc.at[:, t, core]
        send(half, half, pair(sib_sem, t), sibling)
        copies.expect(("sib", t), half, pair(sib_sem, t))

    for t in range(2):
        for j in range(NLO):
            left, right = first[j, 0].astype(F32), first[j, 1].astype(F32)
            rows = jnp.concatenate([left[8 * t : 8 * t + 8], right[8 * t : 8 * t + 8]], axis=0)
            lanes[t, :, 112 * j : 112 * (j + 1)] = rows[:, 0:112]
        hc[x, t, core, y] = lanes[t].astype(BF16)
        if t == 0:
            share(0)
    gathered(0)
    copies.arrive(("pre", 1))
    total = [None, None]
    for c in range(NX):
        states = hc[c, 0, core].reshape(64, 896)
        states = jnp.concatenate([states, states], axis=0)
        for s in range(2):
            term = lax.dot_general(
                table[s, :, 896 * c : 896 * (c + 1)], states, CONTRACT_LAST, preferred_element_type=F32
            )
            total[s] = term if c == 0 else total[s] + term
    peak = jnp.max(jnp.maximum(total[0], total[1]), axis=0, keepdims=True)
    p = [jnp.exp(t - peak) for t in total]
    gap = [t - teach_ref[s] for s, t in enumerate(total)]
    chip_sum = jnp.sum(p[0] + p[1], axis=0, keepdims=True)
    chip_cross = jnp.sum(p[0] * gap[0] + p[1] * gap[1], axis=0, keepdims=True)
    stat_xy[me] = tile_of([peak, chip_sum, chip_cross, top_t, total_t])
    sems = pair(st_sem, 0)
    for x_, y_ in in_plane:
        send(stat_xy.at[me], stat_xy.at[me], sems, device(x_, y_, z, core))
    copies.expect("st1", stat_xy.at[0 : NXY - 1], sems)
    logits_ref[0] = total[0]
    logits_ref[1] = total[1]

    mean = chip_cross / chip_sum
    both = [
        jnp.where(left_lanes(p[s].shape), p[s] * (gap[s] - mean), p[s]).astype(BF16) for s in range(2)
    ]
    sems = pair(rs1_sem)
    for i, c in enumerate([lax.rem(x + i, NX) for i in (2, 1, 3, 0)]):
        at = pl.ds(pl.multiple_of(896 * c, 128), 896)
        sums = lax.dot_general(both[0], table[0, :, at], CONTRACT_FIRST, preferred_element_type=F32)
        sums = sums + lax.dot_general(both[1], table[1, :, at], CONTRACT_FIRST, preferred_element_type=F32)
        sums = sums.astype(BF16).reshape(2, NY, 16, 896)
        for r in range(NY):
            for k in range(2):
                t_ref[i, r, k] = sums[k, r]
        for j in (2, 1, 3, 0):
            y_ = lax.rem(y + j, NY)
            if i < 3 or j > 0:
                send(t_ref.at[i, y_], u_ref.at[me], sems, device(c, y_, z, core))
            else:
                u_ref[me] = t_ref[i, y_]
    copies.expect("rs1", u_ref.at[0 : NXY - 1], sems)
    share(1)

    copies.arrive("st1")
    stat_z[z] = tile_of(merge_tiles(stat_xy))
    sems = pair(st_sem, 1)
    for z_ in along_z:
        send(stat_z.at[z], stat_z.at[z], sems, device(x, y, z_, core))
    copies.expect("st2", stat_z.at[0 : NZ - 1], sems)
    to_sibling(0)
    copies.arrive("st2")
    peak_s, sum_s, cross, peak_t, sum_t = merge_tiles(stat_z)

    log_zs = peak_s + jnp.log(sum_s)
    log_zt = peak_t + jnp.log(sum_t)
    kl_term = cross / sum_s - log_zs + log_zt
    part = jnp.sum(jnp.where(left_lanes(weight.shape), weight * kl_term, 0.0), axis=1, keepdims=True)
    scale = weight / sum_s * jnp.exp(stat_xy[:, 0, :] - peak_s)
    shift = scale * (stat_xy[:, 2, :] / stat_xy[:, 1, :] - cross / sum_s)
    cols_ref[...] = jnp.concatenate([scale, shift, jnp.zeros((128 - 2 * NXY, 128), F32)], axis=0).T
    cols = cols_ref[pl.ds(pl.multiple_of(y * 16, 16), 16), :]

    copies.arrive("rs1")
    acc = jnp.zeros((16, 896), F32)
    for j in range(NXY):
        acc = acc + cols[:, j : j + 1] * u_ref[j, 0].astype(F32)
        acc = acc + cols[:, NXY + j : NXY + j + 1] * u_ref[j, 1].astype(F32)
    lanes[0] = acc
    z_src[...] = jnp.zeros_like(z_src)
    for j in range(NLO):
        for k in range(NCORE):
            z_src[j, k, :, 0:112] = lanes[0, 8 * k : 8 * k + 8, 112 * j : 112 * (j + 1)]

    sems = pair(rs2_sem)
    for j in (0, 7, 1, 6, 2, 5, 3, 4):
        lo_ = lax.rem(lo + j, NLO)
        send(z_src.at[lo_, other], z_dst.at[z], sems, device(x, y, core * NLO + lo_, other))
        if j > 0:
            send(z_src.at[lo_, core], z_dst.at[z], sems, device(x, y, core * NLO + lo_, core))
        else:

            @pl.when(core == hi)
            def _():
                pltpu.make_async_copy(z_src.at[lo, core], z_dst.at[z], sems[1]).start()

            @pl.when(core != hi)
            def _():
                send(z_src.at[lo, core], z_dst.at[z], sems, device(x, y, core * NLO + lo, core))

    def logits_grad(s):
        logits = logits_ref[s]
        inner = jnp.exp(logits - log_zs) * (logits - teach_ref[s] - log_zs + log_zt - kl_term)
        return (weight * inner).astype(BF16)

    loss_x[core] = jnp.broadcast_to(part, (8, 128))
    g_out[...] = logits_grad(other)
    for i, (src, dst) in enumerate(((g_out, g_all.at[core]), (loss_x.at[core], loss_x.at[core]))):
        send(src, dst, pair(g_sem, i), sibling)
        copies.expect(("g", i), dst, pair(g_sem, i))
    own = logits_grad(core)
    gathered(1)
    to_sibling(1)
    ids = ids_in[...]
    ids = jnp.concatenate([ids[:, 32 * q + 16 * h : 32 * q + 16 * h + 16] for h in range(2) for q in range(NY)], axis=1)
    rows = own.shape[0]
    entries = (section * (NY * NHI * NCORE) + fsdp) * rows + lax.broadcasted_iota(jnp.int32, (rows, 128), 0)
    selector = (entries == ids).astype(BF16)
    for i in range(2):
        copies.arrive(("g", i))
    for t in range(2):
        copies.arrive(("sib", t))
    loss_ref[...] = loss_x[0, 0:1] + loss_x[1, 0:1]
    mine = left_lanes(own.shape) == (core == 0)
    glog = jnp.where(mine, own.astype(F32), g_all[other].astype(F32)).astype(BF16)
    both = jnp.concatenate([glog, selector], axis=1)
    for c in range(NX):
        grad_ref[:, 896 * c : 896 * (c + 1)] = jnp.dot(
            both, hc[c].reshape(256, 896), preferred_element_type=F32
        ).astype(BF16)
    store = pltpu.make_async_copy(grad_ref, grad_hbm, store_sem)
    store.start()
    copies.wait(z_dst, rs2_sem.at[1])
    state_ref[...] = jnp.sum(z_dst[...], axis=0)[:, 0:112].astype(BF16)

    tiles = first.reshape(NZ, 16, 128)

    @pl.when(core == hi)
    def _():
        copies.wait(tiles.at[0 : NZ - 1], ag1_sem.at[0])
        copies.wait(z_dst.at[0 : NZ - 1], rs2_sem.at[0])

    @pl.when(core != hi)
    def _():
        copies.wait(tiles, ag1_sem.at[0])
        copies.wait(z_dst, rs2_sem.at[0])

    for t in range(2):
        copies.wait(hc.at[0:3, t, 0, 0:4], plane_send.at[t])
        copies.wait(hc.at[0:3, t, 0, 0], plane_send.at[t])
    copies.finish()
    store.wait()


def shards(table, hidden_states, embed_cotangent, teacher_logits, student_ids, loss_mask):
    rows, width = table.shape
    tokens = teacher_logits.shape[1]
    block = hidden_states.shape
    vmem = pl.BlockSpec(memory_space=pltpu.VMEM)
    hbm = pl.BlockSpec(memory_space=pltpu.HBM)
    dma = pltpu.SemaphoreType.DMA
    table_grad, state_grad, loss = pl.pallas_call(
        kernel,
        out_shape=(
            jax.ShapeDtypeStruct((rows, width), BF16),
            jax.ShapeDtypeStruct(block, BF16),
            jax.ShapeDtypeStruct((1, 128), F32),
        ),
        in_specs=[hbm] * 6,
        out_specs=(pl.BlockSpec(memory_space=pl.ANY), vmem, vmem),
        scratch_shapes=[
            pltpu.VMEM((NCORE, rows, width), BF16),
            pltpu.VMEM(block, BF16),
            pltpu.VMEM(block, BF16),
            pltpu.VMEM((NCORE, rows, tokens), BF16),
            pltpu.VMEM((1, 128), jnp.int32),
            pltpu.VMEM((1, 128), jnp.int32),
            pltpu.VMEM((16, 128), BF16),
            pltpu.VMEM((NLO, NCORE, 16, 128), BF16),
            pltpu.VMEM((2, 16, 896), F32),
            pltpu.VMEM((NX, 2, NHI, NY, 16, 896), BF16),
            pltpu.VMEM((NXY, 8, 128), F32),
            pltpu.VMEM((NZ, 8, 128), F32),
            pltpu.VMEM((NCORE, rows, tokens), F32),
            pltpu.VMEM((NCORE, rows, tokens), F32),
            pltpu.VMEM((NX, NY, 2, 16, 896), BF16),
            pltpu.VMEM((NXY, 2, 16, 896), BF16),
            pltpu.VMEM((128, 128), F32),
            pltpu.VMEM((NLO, NCORE, 8, 128), F32),
            pltpu.VMEM((NZ, 8, 128), F32),
            pltpu.VMEM((rows, tokens), BF16),
            pltpu.VMEM((NCORE, rows, tokens), BF16),
            pltpu.VMEM((NCORE, 8, 128), F32),
            pltpu.VMEM((rows, width), BF16),
            dma((6,)),
            dma,
            dma((2,)),
            dma((2, 2)),
            dma((2,)),
            dma((2, NXY)),
            dma((2, 2)),
            dma((2, 2)),
            dma((2,)),
            dma((2,)),
            dma((2, 2)),
        ],
        compiler_params=pltpu.CompilerParams(
            collective_id=0, has_side_effects=True, vmem_limit_bytes=VMEM_MIB * 1024 * 1024
        ),
    )(
        table,
        hidden_states,
        embed_cotangent,
        teacher_logits,
        student_ids.reshape(1, 128),
        loss_mask.reshape(1, 128),
    )
    return table_grad, state_grad, loss[0, 0]


def solution(mesh):
    return jax.shard_map(
        shards,
        mesh=mesh,
        in_specs=(
            P(("section", "fsdp"), None),
            P("fsdp", "section"),
            P("fsdp", "section"),
            P(("section", "fsdp"), None),
            P(),
            P(),
        ),
        out_specs=(P(("section", "fsdp"), None), P("fsdp", "section"), P()),
        check_vma=False,
    )
```

time: 65.9 us -> 63.3 us (0.961)
  Pallas kernels: 60.5 us -> 57.9 us
    pallas_call x1, Pallas kernels: 60.5 us -> 57.9 us  [shards(): pl.pallas_call(kernel, out_shape=(jax.ShapeDtypeStruct((rows, width), BF1...]
where the time goes in v3:
time: 63.3 us; the launch traced here: 63.1 us
  Pallas kernels  57.9 us (91%)
  local copies, waits for them, and re-layouts  3.43 us (5%)
  between operations  1.82 us (3%)
    pallas_call x1, Pallas kernels, shards(): pl.pallas_call(kernel, out_shape=(jax.ShapeDtypeStruct((rows, width), BF1...  57.9 us
    unnamed x6, local copies, waits for them, and re-layouts  3.43 us

profile of v3, /device:TPU:1, one launch (start us, length us, event | category | flops | bytes accessed | tf_op | source)
XLA Modules:
  0.0 63.1 jit_solution(13417259598687192329)
XLA Ops:
  0.6 57.9 %shard_map.85 = (bf16[250,3584]{1,0:T(8,128)(2,1)}, bf16[8,112]{1,0:T(8,128)(2,1)}, f32[1,128]{1,0:T(1,128)}) custom-call(bf16[250,3584]{1,0:T(8,128)(2,1)} %table_hbm.1, bf16[8,112]{1,0:T(8,128)(2,1)} %hidden_hbm.1, bf16[8,112]{1,0:T(8,128)(2,1)} %cot_hbm.1, bf16[250,128]{1,0:T(8,128)(2,1)} %teach_hbm.1, s32[1,128]{1,0:T(1,128)} %bitcast.4, s32[1,128]{1,0:T(1,128)} %bitcast.5), custom_call_target="tpu_custom_call" | custom-call | tf_op jit(solution)/shard_map/pallas_call | solution.py:334
  58.5 0.0 copy-start
  58.5 0.0 copy-start.1
  58.5 2.8 %copy.12 = bf16[250,3584]{1,0:T(8,128)(2,1)} copy(bf16[250,3584]{1,0:T(8,128)(2,1)} %get-tuple-element.12) | data formatting | bytes 3584000
  61.4 0.0 copy-done
  61.4 0.6 copy.13
  61.9 0.0 copy-done.1
Async XLA Ops:
  58.5 2.9 %copy-start = (bf16[8,112]{1,0:T(8,128)(2,1)S(1)}, bf16[8,112]{1,0:T(8,128)(2,1)}, u32[]{:S(2)}) copy-start(bf16[8,112]{1,0:T(8,128)(2,1)} %get-tuple-element.13) | copy-start | bytes 5380
  58.5 3.4 %copy-start.1 = (f32[1,128]{1,0:T(1,128)S(1)}, f32[1,128]{1,0:T(1,128)}, u32[]{:S(2)}) copy-start(f32[1,128]{1,0:T(1,128)} %get-tuple-element.8) | copy-start | bytes 1540

commit v4 on v3

--- a/solution.py
+++ b/solution.py
@@ -178,17 +178,20 @@
         hc[x, t, core, y] = lanes[t].astype(BF16)
         if t == 0:
             share(0)
-    gathered(0)
     copies.arrive(("pre", 1))
     total = [None, None]
-    for c in range(NX):
+    for i in (0, 1, 3, 2):
+        c = lax.rem(x + i, NX)
+        for j in (0, 1, 3, 2):
+            if i or j:
+                y_ = lax.rem(y + j, NY)
+                copies.wait(hc.at[c, 0, core, y_], plane_recv.at[0, c * NY + y_])
         states = hc[c, 0, core].reshape(64, 896)
         states = jnp.concatenate([states, states], axis=0)
+        at = pl.ds(pl.multiple_of(896 * c, 128), 896)
         for s in range(2):
-            term = lax.dot_general(
-                table[s, :, 896 * c : 896 * (c + 1)], states, CONTRACT_LAST, preferred_element_type=F32
-            )
-            total[s] = term if c == 0 else total[s] + term
+            term = lax.dot_general(table[s, :, at], states, CONTRACT_LAST, preferred_element_type=F32)
+            total[s] = term if i == 0 else total[s] + term
     peak = jnp.max(jnp.maximum(total[0], total[1]), axis=0, keepdims=True)
     p = [jnp.exp(t - peak) for t in total]
     gap = [t - teach_ref[s] for s, t in enumerate(total)]
@@ -322,6 +325,20 @@
         copies.wait(hc.at[0:3, t, 0, 0], plane_send.at[t])
     copies.finish()
     store.wait()
+
+
+def hand_over(grad, state, loss, grad_out, state_out, loss_out, grad_v, state_v, loss_v, in_sem, out_sem):
+    parts = [(grad.at[:, at], grad_v.at[:, at], grad_out.at[:, at]) for at in (pl.ds(896 * c, 896) for c in range(NX))]
+    parts = [(state, state_v, state_out), (loss, loss_v, loss_out), *parts]
+    loads = [pltpu.make_async_copy(src, via, in_sem.at[i]) for i, (src, via, _) in enumerate(parts)]
+    stores = [pltpu.make_async_copy(via, dst, out_sem.at[i]) for i, (_, via, dst) in enumerate(parts)]
+    for load in loads:
+        load.start()
+    for load, store in zip(loads, stores):
+        load.wait()
+        store.start()
+    for store in stores:
+        store.wait()
 
 
 def shards(table, hidden_states, embed_cotangent, teacher_logits, student_ids, loss_mask):
@@ -387,6 +404,15 @@
         student_ids.reshape(1, 128),
         loss_mask.reshape(1, 128),
     )
+    results = (table_grad, state_grad, loss)
+    table_grad, state_grad, loss = pl.pallas_call(
+        hand_over,
+        out_shape=[jax.ShapeDtypeStruct(r.shape, r.dtype) for r in results],
+        in_specs=[pl.BlockSpec(memory_space=pl.ANY)] * 3,
+        out_specs=[pl.BlockSpec(memory_space=pl.ANY)] * 3,
+        scratch_shapes=[*(pltpu.VMEM(r.shape, r.dtype) for r in results), dma((NX + 2,)), dma((NX + 2,))],
+        compiler_params=pltpu.CompilerParams(vmem_limit_bytes=VMEM_MIB * 1024 * 1024),
+    )(*results)
     return table_grad, state_grad, loss[0, 0]
 
 

time: 63.3 us -> 60.7 us (0.959)
  local copies, waits for them, and re-layouts: 3.43 us -> 0 us
  Pallas kernels: 57.9 us -> 59.5 us
  between operations: 1.82 us -> 0.64 us
    unnamed x6 -> x0, local copies, waits for them, and re-layouts: 3.43 us -> none
    pallas_call x0 -> x1, Pallas kernels: none -> 2.35 us  [shards(): pl.pallas_call(hand_over, out_shape=[jax.ShapeDtypeStruct(r.shape, r.dtyp...]
    pallas_call x1, Pallas kernels: 57.9 us -> 57.1 us  [shards(): pl.pallas_call(kernel, out_shape=(jax.ShapeDtypeStruct((rows, width), BF1...]
where the time goes in v4:
time: 60.7 us; the launch traced here: 60.1 us
  Pallas kernels  59.5 us (98%)
  between operations  0.64 us (1%)
    pallas_call x1, Pallas kernels, shards(): pl.pallas_call(kernel, out_shape=(jax.ShapeDtypeStruct((rows, width), BF1...  57.1 us
    pallas_call x1, Pallas kernels, shards(): pl.pallas_call(hand_over, out_shape=[jax.ShapeDtypeStruct(r.shape, r.dtyp...  2.35 us

profile of v4, /device:TPU:1, one launch (start us, length us, event | category | flops | bytes accessed | tf_op | source)
XLA Modules:
  0.0 60.1 jit_solution(8124456177756430933)
XLA Ops:
  0.6 57.1 %shard_map.85 = (bf16[250,3584]{1,0:T(8,128)(2,1)}, bf16[8,112]{1,0:T(8,128)(2,1)}, f32[1,128]{1,0:T(1,128)}) custom-call(bf16[250,3584]{1,0:T(8,128)(2,1)} %table_hbm.1, bf16[8,112]{1,0:T(8,128)(2,1)} %hidden_hbm.1, bf16[8,112]{1,0:T(8,128)(2,1)} %cot_hbm.1, bf16[250,128]{1,0:T(8,128)(2,1)} %teach_hbm.1, s32[1,128]{1,0:T(1,128)} %bitcast.4, s32[1,128]{1,0:T(1,128)} %bitcast.5), custom_call_target="tpu_custom_call" | custom-call | tf_op jit(solution)/shard_map/pallas_call | solution.py:351
  57.8 2.4 %shard_map.86 = (bf16[250,3584]{1,0:T(8,128)(2,1)}, bf16[8,112]{1,0:T(8,128)(2,1)}, f32[1,128]{1,0:T(1,128)}) custom-call(bf16[250,3584]{1,0:T(8,128)(2,1)} %get-tuple-element.9.grad, bf16[8,112]{1,0:T(8,128)(2,1)} %get-tuple-element.10.state, f32[1,128]{1,0:T(1,128)} %get-tuple-element.11.loss), custom_call_target="tpu_custom_call" | custom-call | tf_op jit(solution)/shard_map/pallas_call | solution.py:408

commit v5 on v4

--- a/solution.py
+++ b/solution.py
@@ -28,13 +28,11 @@
 
 
 def merge_tiles(ref):
-    peak_s, sum_s, cross = merge(ref[:, 0, :], ref[:, 1, :], ref[:, 2, :])
-    peak_t, sum_t = merge(ref[:, 3, :], ref[:, 4, :])
-    return peak_s, sum_s, cross, peak_t, sum_t
+    return merge(ref[:, 0, :], ref[:, 1, :], ref[:, 2, :])
 
 
 def tile_of(rows):
-    return jnp.concatenate([*rows, jnp.zeros((3, rows[0].shape[1]), F32)], axis=0)
+    return jnp.concatenate([*rows, jnp.zeros((1, 128), F32)], axis=0)
 
 
 class Copies:
@@ -197,7 +195,8 @@
     gap = [t - teach_ref[s] for s, t in enumerate(total)]
     chip_sum = jnp.sum(p[0] + p[1], axis=0, keepdims=True)
     chip_cross = jnp.sum(p[0] * gap[0] + p[1] * gap[1], axis=0, keepdims=True)
-    stat_xy[me] = tile_of([peak, chip_sum, chip_cross, top_t, total_t])
+    left = left_lanes(peak.shape)
+    stat_xy[me] = tile_of([jnp.where(left, peak, top_t), jnp.where(left, chip_sum, total_t), jnp.where(left, chip_cross, 0.0)])
     sems = pair(st_sem, 0)
     for x_, y_ in in_plane:
         send(stat_xy.at[me], stat_xy.at[me], sems, device(x_, y_, z, core))
@@ -225,7 +224,6 @@
             else:
                 u_ref[me] = t_ref[i, y_]
     copies.expect("rs1", u_ref.at[0 : NXY - 1], sems)
-    share(1)
 
     copies.arrive("st1")
     stat_z[z] = tile_of(merge_tiles(stat_xy))
@@ -233,9 +231,13 @@
     for z_ in along_z:
         send(stat_z.at[z], stat_z.at[z], sems, device(x, y, z_, core))
     copies.expect("st2", stat_z.at[0 : NZ - 1], sems)
+    share(1)
     to_sibling(0)
     copies.arrive("st2")
-    peak_s, sum_s, cross, peak_t, sum_t = merge_tiles(stat_z)
+    merged = merge_tiles(stat_z)
+    swapped = [jnp.concatenate([v[:, 64:128], v[:, 0:64]], axis=1) for v in merged]
+    peak_s, sum_s, cross = (jnp.where(left, v, w) for v, w in zip(merged, swapped, strict=True))
+    peak_t, sum_t = (jnp.where(left, w, v) for v, w in zip(merged[:2], swapped[:2], strict=True))
 
     log_zs = peak_s + jnp.log(sum_s)
     log_zt = peak_t + jnp.log(sum_t)
@@ -368,8 +370,8 @@
             pltpu.VMEM((NLO, NCORE, 16, 128), BF16),
             pltpu.VMEM((2, 16, 896), F32),
             pltpu.VMEM((NX, 2, NHI, NY, 16, 896), BF16),
-            pltpu.VMEM((NXY, 8, 128), F32),
-            pltpu.VMEM((NZ, 8, 128), F32),
+            pltpu.VMEM((NXY, 4, 128), F32),
+            pltpu.VMEM((NZ, 4, 128), F32),
             pltpu.VMEM((NCORE, rows, tokens), F32),
             pltpu.VMEM((NCORE, rows, tokens), F32),
             pltpu.VMEM((NX, NY, 2, 16, 896), BF16),

time: 60.7 us -> 59.9 us (0.987)
  no operation moved by 1% of the time
where the time goes in v5:
time: 59.9 us; the launch traced here: 59.8 us
  Pallas kernels  59.1 us (99%)
  between operations  0.64 us (1%)
    pallas_call x1, Pallas kernels, shards(): pl.pallas_call(kernel, out_shape=(jax.ShapeDtypeStruct((rows, width), BF1...  56.8 us
    pallas_call x1, Pallas kernels, shards(): pl.pallas_call(hand_over, out_shape=[jax.ShapeDtypeStruct(r.shape, r.dtyp...  2.35 us

profile of v5, /device:TPU:1, one launch (start us, length us, event | category | flops | bytes accessed | tf_op | source)
XLA Modules:
  0.0 59.8 jit_solution(17809810824355685273)
XLA Ops:
  0.6 56.8 %shard_map.85 = (bf16[250,3584]{1,0:T(8,128)(2,1)}, bf16[8,112]{1,0:T(8,128)(2,1)}, f32[1,128]{1,0:T(1,128)}) custom-call(bf16[250,3584]{1,0:T(8,128)(2,1)} %table_hbm.1, bf16[8,112]{1,0:T(8,128)(2,1)} %hidden_hbm.1, bf16[8,112]{1,0:T(8,128)(2,1)} %cot_hbm.1, bf16[250,128]{1,0:T(8,128)(2,1)} %teach_hbm.1, s32[1,128]{1,0:T(1,128)} %bitcast.4, s32[1,128]{1,0:T(1,128)} %bitcast.5), custom_call_target="tpu_custom_call" | custom-call | tf_op jit(solution)/shard_map/pallas_call | solution.py:353
  57.4 2.4 %shard_map.86 = (bf16[250,3584]{1,0:T(8,128)(2,1)}, bf16[8,112]{1,0:T(8,128)(2,1)}, f32[1,128]{1,0:T(1,128)}) custom-call(bf16[250,3584]{1,0:T(8,128)(2,1)} %get-tuple-element.9.grad, bf16[8,112]{1,0:T(8,128)(2,1)} %get-tuple-element.10.state, f32[1,128]{1,0:T(1,128)} %get-tuple-element.11.loss), custom_call_target="tpu_custom_call" | custom-call | tf_op jit(solution)/shard_map/pallas_call | solution.py:410

commit v6 on v5

--- a/solution.py
+++ b/solution.py
@@ -233,18 +233,16 @@
     copies.expect("st2", stat_z.at[0 : NZ - 1], sems)
     share(1)
     to_sibling(0)
+    z_src[...] = jnp.zeros_like(z_src)
+    means = stat_xy[:, 2, :] / stat_xy[:, 1, :]
     copies.arrive("st2")
     merged = merge_tiles(stat_z)
     swapped = [jnp.concatenate([v[:, 64:128], v[:, 0:64]], axis=1) for v in merged]
     peak_s, sum_s, cross = (jnp.where(left, v, w) for v, w in zip(merged, swapped, strict=True))
     peak_t, sum_t = (jnp.where(left, w, v) for v, w in zip(merged[:2], swapped[:2], strict=True))
 
-    log_zs = peak_s + jnp.log(sum_s)
-    log_zt = peak_t + jnp.log(sum_t)
-    kl_term = cross / sum_s - log_zs + log_zt
-    part = jnp.sum(jnp.where(left_lanes(weight.shape), weight * kl_term, 0.0), axis=1, keepdims=True)
     scale = weight / sum_s * jnp.exp(stat_xy[:, 0, :] - peak_s)
-    shift = scale * (stat_xy[:, 2, :] / stat_xy[:, 1, :] - cross / sum_s)
+    shift = scale * (means - cross / sum_s)
     cols_ref[...] = jnp.concatenate([scale, shift, jnp.zeros((128 - 2 * NXY, 128), F32)], axis=0).T
     cols = cols_ref[pl.ds(pl.multiple_of(y * 16, 16), 16), :]
 
@@ -254,7 +252,6 @@
         acc = acc + cols[:, j : j + 1] * u_ref[j, 0].astype(F32)
         acc = acc + cols[:, NXY + j : NXY + j + 1] * u_ref[j, 1].astype(F32)
     lanes[0] = acc
-    z_src[...] = jnp.zeros_like(z_src)
     for j in range(NLO):
         for k in range(NCORE):
             z_src[j, k, :, 0:112] = lanes[0, 8 * k : 8 * k + 8, 112 * j : 112 * (j + 1)]
@@ -274,6 +271,11 @@
             @pl.when(core != hi)
             def _():
                 send(z_src.at[lo, core], z_dst.at[z], sems, device(x, y, core * NLO + lo, core))
+
+    log_zs = peak_s + jnp.log(sum_s)
+    log_zt = peak_t + jnp.log(sum_t)
+    kl_term = cross / sum_s - log_zs + log_zt
+    part = jnp.sum(jnp.where(left_lanes(weight.shape), weight * kl_term, 0.0), axis=1, keepdims=True)
 
     def logits_grad(s):
         logits = logits_ref[s]

time: 59.9 us -> 59.9 us (level)
  no operation moved by 1% of the time
where the time goes in v6:
time: 59.9 us; the launch traced here: 59.8 us
  Pallas kernels  59.1 us (99%)
  between operations  0.64 us (1%)
    pallas_call x1, Pallas kernels, shards(): pl.pallas_call(kernel, out_shape=(jax.ShapeDtypeStruct((rows, width), BF1...  56.8 us
    pallas_call x1, Pallas kernels, shards(): pl.pallas_call(hand_over, out_shape=[jax.ShapeDtypeStruct(r.shape, r.dtyp...  2.35 us

profile of v6, /device:TPU:1, one launch (start us, length us, event | category | flops | bytes accessed | tf_op | source)
XLA Modules:
  0.0 59.8 jit_solution(6660672735266580954)
XLA Ops:
  0.6 56.8 %shard_map.85 = (bf16[250,3584]{1,0:T(8,128)(2,1)}, bf16[8,112]{1,0:T(8,128)(2,1)}, f32[1,128]{1,0:T(1,128)}) custom-call(bf16[250,3584]{1,0:T(8,128)(2,1)} %table_hbm.1, bf16[8,112]{1,0:T(8,128)(2,1)} %hidden_hbm.1, bf16[8,112]{1,0:T(8,128)(2,1)} %cot_hbm.1, bf16[250,128]{1,0:T(8,128)(2,1)} %teach_hbm.1, s32[1,128]{1,0:T(1,128)} %bitcast.4, s32[1,128]{1,0:T(1,128)} %bitcast.5), custom_call_target="tpu_custom_call" | custom-call | tf_op jit(solution)/shard_map/pallas_call | solution.py:355
  57.4 2.4 %shard_map.86 = (bf16[250,3584]{1,0:T(8,128)(2,1)}, bf16[8,112]{1,0:T(8,128)(2,1)}, f32[1,128]{1,0:T(1,128)}) custom-call(bf16[250,3584]{1,0:T(8,128)(2,1)} %get-tuple-element.9.grad, bf16[8,112]{1,0:T(8,128)(2,1)} %get-tuple-element.10.state, f32[1,128]{1,0:T(1,128)} %get-tuple-element.11.loss), custom_call_target="tpu_custom_call" | custom-call | tf_op jit(solution)/shard_map/pallas_call | solution.py:412
